TPU v7x, 32 devices: a whole 2x2x4 slice. The times are simulated.
32 devices in a mesh: dp: 2 (over x), orient: 16 (over z, y, core).
Axes of the slice: x: 2, y: 2, z: 4, core: 2. Of those that a mesh axis runs over, the one named last changes fastest.
Arguments:
- images: bfloat16 [384, 16384], P(('dp', 'orient')), may hold values from -80 to 80
- templates: bfloat16 [4096, 16384], P('orient'), as said below
- index: int32 [4096, 128], P('orient'), may hold values from 0 to 16383
- interp: float32 [4096, 128], P('orient'), may hold values from 0.25 to 1
- inv_noise: float32 [128, 128], replicated, may hold values from 0.5 to 2, as said below
Outputs:
- recon: float32 [16384, 128], P(('dp', 'orient'))
- recon_weight: float32 [16384, 128], P(('dp', 'orient'))
Inputs may be any that keep to these rules, and one draw needn't show every extreme that they name: `templates`: every entry has magnitude at most 18 / 128. `inv_noise`: every entry is 0.5, 1 or 2.
All inputs are finite; a program needn't handle non-finite values.
Results may differ from a plain program's by a relative error of at most 0.0029.
Values may be sent and summed in bfloat16 or wider, within the bound.
A program may use at most 128 MiB of HBM per device.

v0:
```python
import jax
import jax.numpy as jnp
from jax import lax
from jax.sharding import PartitionSpec as P


def shards(images, templates, index, interp, inv_noise):
    side = inv_noise.shape[0]
    count_tpl = templates.shape[0]
    noise_flat = inv_noise.reshape(-1)
    tpl_f = templates.astype(jnp.float32)
    weighted = (tpl_f * noise_flat[None, :]).astype(jnp.bfloat16)
    tnorm = 0.5 * jnp.sum(tpl_f * tpl_f * noise_flat[None, :], axis=1)
    gathered = lax.all_gather(images, "orient", axis=0, tiled=True)
    scores = (
        lax.dot_general(
            gathered, weighted, (((1,), (1,)), ((), ())), preferred_element_type=jnp.float32
        )
        - tnorm[None, :]
    )
    peak = lax.pmax(jnp.max(scores, axis=1), "orient")
    expo = jnp.exp(scores - peak[:, None])
    total = lax.psum(jnp.sum(expo, axis=1), "orient")
    posterior = expo / total[:, None]
    post_b = posterior.astype(jnp.bfloat16)
    mass = jnp.sum(posterior, axis=0)
    sums = lax.dot_general(
        post_b, gathered, (((0,), (0,)), ((), ())), preferred_element_type=jnp.float32
    )
    rows_idx = index.reshape(-1)
    data_rows = sums.reshape(count_tpl * side, side) * interp.reshape(-1, 1)
    data_vol = jnp.zeros((side * side, side), jnp.float32).at[rows_idx].add(data_rows)
    weight_rows = ((interp * mass[:, None])[:, :, None] * inv_noise[None, :, :]).reshape(
        count_tpl * side, side
    )
    weight_vol = jnp.zeros((side * side, side), jnp.float32).at[rows_idx].add(weight_rows)
    volume = jnp.concatenate([data_vol, weight_vol], axis=1)
    owned = lax.psum_scatter(volume, ("dp", "orient"), scatter_dimension=0, tiled=True)
    return (owned[:, :side], owned[:, side:])


def solution(mesh):
    placed = (
        P(("dp", "orient"), None),
        P("orient", None),
        P("orient", None),
        P("orient", None),
        P(),
    )
    return jax.shard_map(
        shards,
        mesh=mesh,
        in_specs=placed,
        out_specs=(P(("dp", "orient"), None), P(("dp", "orient"), None)),
        check_vma=False,
    )
```

profile of v0, /device:TPU:0, one launch (start us, length us, event | category | flops | bytes accessed | tf_op | source)
XLA Modules:
  0.0 777.0 jit_solution(3466400453175574872)
XLA Ops:
  7.2 0.0 copy-start.1
  7.2 0.0 all-gather.3.cloned.1.call-start
  7.2 0.7 all-gather.3.cloned.1.call-update
  7.9 0.0 reduce-scatter.2.cloned.1.call-start
  8.0 5.7 fusion.2
  13.6 1.0 compare_select_fusion
  14.7 73.1 %all-gather.3.cloned.1.call-done = bf16[16,12,16384]{2,1,0:T(8,128)(2,1)} async-done(((bf16[1,12,16384]{2,1,0:T(8,128)(2,1)}), bf16[16,12,16384]{2,1,0:T(8,128)(2,1)}) %all-gather.3.cloned.1.call-update) | async-done | bytes 6291472 | tf_op jit(solution)/shard_map/all_gather | solution.py:14
  87.8 8.8 %reshape.72 = bf16[192,16384]{1,0:T(8,128)(2,1)} reshape(bf16[16,12,16384]{2,1,0:T(8,128)(2,1)} %all-gather.3.cloned.1.call-done) | data formatting | bytes 12582912
  96.6 0.0 copy-done.1
  96.6 8.2 %fusion.22 = (f32[192]{0:T(256)S(1)}, f32[256,192]{0,1:T(8,128)S(1)}) fusion(f32[256]{0:T(256)S(1)} %broadcast_multiply_fusion, bf16[192,16384]{1,0:T(8,128)(2,1)} %reshape.72, bf16[256,16384]{1,0:T(8,128)(2,1)} %param.6, f32[16384]{0:T(1024)S(1)} %bitcast.14), kind=kOutput, calls=%fused_computation.28 | convolution fusion | flops 1623293696 | bytes 14944000 | tf_op jit(solution)/shard_map/dot_general | solution.py:16
  104.8 31.0 %pmax.7 = f32[192]{0:T(256)S(1)} all-reduce(f32[192]{0:T(256)S(1)} %get-tuple-element.4), channel_id=1, replica_groups=mesh['dp'=2,'orient'=16] {'orient'}, use_global_device_ids=true, to_apply=%region_2.0 | all-reduce | flops 192 | bytes 1536 | tf_op jit(solution)/shard_map/pmax | solution.py:21
  135.7 0.2 fusion.16
  135.9 29.5 %psum.7 = f32[192]{0:T(256)S(1)} all-reduce(f32[192]{0:T(256)S(1)} %fusion.16), channel_id=1, replica_groups=mesh['dp'=2,'orient'=16] {'orient'}, use_global_device_ids=true, to_apply=%region_4.0 | all-reduce | flops 192 | bytes 1536 | tf_op jit(solution)/shard_map/psum | solution.py:23
  165.4 11.0 %fusion.17 = f32[256,16384]{1,0:T(8,128)} fusion(bf16[192,16384]{1,0:T(8,128)(2,1)} %reshape.72, f32[256,192]{0,1:T(8,128)S(1)} %get-tuple-element.5, f32[192]{0:T(256)S(1)} %psum.7, f32[192]{0:T(256)S(1)} %pmax.7), kind=kOutput, calls=%fused_computation.23 | convolution fusion | flops 1610760192 | bytes 23266816 | tf_op jit(solution)/shard_map/dot_general | solution.py:27
  176.4 0.1 fusion.19
  176.6 0.0 copy-start
  176.6 18.1 %reshape.54 = f32[32768,128]{1,0:T(8,128)} reshape(f32[256,16384]{1,0:T(8,128)} %fusion.17) | data formatting | bytes 33554432 | tf_op jit(solution)/shard_map/reshape | solution.py:31
  194.6 0.0 copy-done
  194.6 0.1 multiply_bitcast_fusion
  194.7 8.5 %bitcast_multiply_fusion = f32[32768,128]{1,0:T(8,128)} fusion(f32[128,128]{1,0:T(8,128)S(1)} %copy-done.1, f32[32768]{0:T(1024)S(1)} %multiply_bitcast_fusion), kind=kLoop, calls=%fused_computation.8 | loop fusion | flops 4194304 | bytes 16973824 | tf_op jit(solution)/shard_map/mul | solution.py:33
  203.2 177.9 %scatter_custom_fusion.1 = f32[16384,128]{1,0:T(8,128)} fusion(s32[32768]{0:T(1024)S(1)} %bitcast.16, f32[32768,128]{1,0:T(8,128)} %bitcast_multiply_fusion, f32[]{:T(128)} %constant.5.clone.1), kind=kCustom, calls=%fused_computation.14 | custom fusion | flops 4194304 | bytes 8389120 | tf_op jit(solution)/shard_map/scatter-add | solution.py:36
  381.1 194.9 %scatter_custom_fusion = f32[16384,128]{1,0:T(8,128)} fusion(s32[32768]{0:T(1024)S(1)} %bitcast.17, f32[32768,128]{1,0:T(8,128)} %reshape.54, f32[32768]{0:T(1024)S(1)} %bitcast.11, f32[]{:T(128)} %constant.5.clone.1), kind=kCustom, calls=%fused_computation.9 | custom fusion | flops 8388608 | bytes 25296900 | tf_op jit(solution)/shard_map/scatter-add | solution.py:32
  576.0 11.3 %pad_maximum_fusion = f32[16384,256]{1,0:T(8,128)} fusion(f32[16384,128]{1,0:T(8,128)} %scatter_custom_fusion.1, f32[16384,128]{1,0:T(8,128)} %scatter_custom_fusion), kind=kLoop, calls=%fused_computation.7 | loop fusion | flops 4194304 | bytes 33554432 | tf_op jit(solution)/shard_map/concatenate | solution.py:37
  587.3 0.0 reduce-scatter.2.cloned.1.call-update
  587.3 181.0 %reduce-scatter.2.cloned.1.call-done = f32[512,256]{1,0:T(8,128)} async-done(((f32[16384,256]{1,0:T(8,128)}), f32[512,256]{1,0:T(8,128)}) %reduce-scatter.2.cloned.1.call-update) | async-done | bytes 524304 | tf_op jit(solution)/shard_map/reduce_scatter | solution.py:38
  768.3 1.9 fusion.21
  (1 shorter events, 0.0 us)
Async XLA Ops:
  7.2 89.4 %copy-start.1 = (f32[128,128]{1,0:T(8,128)S(1)}, f32[128,128]{1,0:T(8,128)}, u32[]{:S(2)}) copy-start(f32[128,128]{1,0:T(8,128)} %param.9) | copy-start | bytes 196612
  7.2 80.6 %all-gather.3.cloned.1.call-start = ((), (), s32[]{:S(2)}) async-start(), calls=%async_computation.2 | async-start | bytes 8912896 | tf_op jit(solution)/shard_map/all_gather | solution.py:14
  7.9 760.4 %reduce-scatter.2.cloned.1.call-start = ((), (), s32[]{:S(2)}) async-start(), calls=%async_computation.1 | async-start | bytes 17301504 | tf_op jit(solution)/shard_map/reduce_scatter | solution.py:38
  176.6 18.1 %copy-start = (f32[256,128]{1,0:T(8,128)S(1)}, f32[256,128]{1,0:T(8,128)}, u32[]{:S(2)}) copy-start(f32[256,128]{1,0:T(8,128)} %param.8) | copy-start | bytes 393220
Sparse Core Ops, SparseCore 0:
  10.2 77.5 all-gather.2
  587.4 180.8 reduce-scatter.1
where the time goes:
time: 778 us; the launch traced here: 777 us
  other arithmetic  400 us (51%)
  waiting for transfers between devices  255 us (33%)
  blocking collectives  60.5 us (8%)
  local copies, waits for them, and re-layouts  28.7 us (4%)
  matrix products  19.2 us (2%)
  between operations  14.1 us (2%)
    scatter-add x1, other arithmetic, shards(): jnp.zeros((side * side, side), jnp.float32).at[rows_idx].add(data_rows)  195 us
    reduce_scatter x1, waiting for transfers between devices, shards(): lax.psum_scatter(volume, ('dp', 'orient'), scatter_dimension=0, tiled=True)  181 us
    scatter-add x1, other arithmetic, shards(): jnp.zeros((side * side, side), jnp.float32).at[rows_idx].add(weight_rows)  178 us
    all_gather x1, waiting for transfers between devices, shards(): gathered = lax.all_gather(images, 'orient', axis=0, tiled=True)  73.1 us
    pmax x1, blocking collectives, shards(): peak = lax.pmax(jnp.max(scores, axis=1), 'orient')  31 us
    psum x1, blocking collectives, shards(): total = lax.psum(jnp.sum(expo, axis=1), 'orient')  29.5 us
    reshape x1, local copies, waits for them, and re-layouts, shards(): data_rows = sums.reshape(count_tpl * side, side) * interp.reshape(-1, 1)  18.1 us
  transfers between devices with their start and end apart: 2, of which 2 were waited for; matrix products, arithmetic and copies ran while one was open for 1% of the time, Pallas kernels for 0%

commit v1 on v0

--- a/solution.py
+++ b/solution.py
@@ -1,7 +1,29 @@
+import functools
 import jax
 import jax.numpy as jnp
 from jax import lax
 from jax.sharding import PartitionSpec as P
+from jax.lax import axis_index, ppermute, psum
+
+
+def start_notes(u_in, mesh_ax):
+    odd, z1, new = (psum(1, mesh_ax), axis_index(mesh_ax), u_in.shape[0])
+    gallery = [(d, (d + 1) % odd) for d in range(odd)]
+    trail = [(d, (d - 1) % odd) for d in range(odd)]
+    e_next = jnp.zeros((*u_in.shape[:0], odd * new, *u_in.shape[1:]), u_in.dtype)
+    e_next = lax.dynamic_update_slice_in_dim(e_next, u_in, z1 * new, axis=0)
+    y = odd // 2
+    clean = ready = u_in
+    for rr in range(1, y + 1):
+        clean = ppermute(clean, mesh_ax, gallery)
+        e_next = lax.dynamic_update_slice_in_dim(e_next, clean, (z1 - rr) % odd * new, axis=0)
+        if rr < odd - y:
+            ready = ppermute(ready, mesh_ax, trail)
+            e_next = lax.dynamic_update_slice_in_dim(e_next, ready, (z1 + rr) % odd * new, axis=0)
+    return e_next
+
+
+remake_the_goods = functools.partial(start_notes, mesh_ax="orient")
 
 
 def shards(images, templates, index, interp, inv_noise):
@@ -11,7 +33,7 @@
     tpl_f = templates.astype(jnp.float32)
     weighted = (tpl_f * noise_flat[None, :]).astype(jnp.bfloat16)
     tnorm = 0.5 * jnp.sum(tpl_f * tpl_f * noise_flat[None, :], axis=1)
-    gathered = lax.all_gather(images, "orient", axis=0, tiled=True)
+    gathered = remake_the_goods(images)
     scores = (
         lax.dot_general(
             gathered, weighted, (((1,), (1,)), ((), ())), preferred_element_type=jnp.float32

time: 778 us -> 873 us (1.12)
  starting transfers between devices: 0.08 us -> 68.6 us
  local copies, waits for them, and re-layouts: 28.7 us -> 96.9 us
  waiting for transfers between devices: 255 us -> 211 us
    dynamic_update_slice x0 -> x16, local copies, waits for them, and re-layouts: none -> 73.6 us  [the longest x8 36.2 us: start_notes(): lax.dynamic_update_slice_in_dim(e_next, clean, (z1 - rr) % odd * new, axi...]
    all_gather x1 -> x0, waiting for transfers between devices: 73.1 us -> none  [shards(): gathered = lax.all_gather(images, 'orient', axis=0, tiled=True)]
    ppermute x0 -> x15, starting transfers between devices: none -> 68.5 us  [the longest x8 61.3 us: start_notes(): clean = ppermute(clean, mesh_ax, gallery)]
    ppermute x0 -> x15, waiting for transfers between devices: none -> 29.4 us  [the longest x8 29.4 us: start_notes(): clean = ppermute(clean, mesh_ax, gallery)]
    unnamed x5 -> x24, local copies, waits for them, and re-layouts: 8.79 us -> 0.05 us
  transfers between devices with their start and end apart: 2 -> 16, of which waited for: 2 -> 8; matrix products, arithmetic and copies ran while one was open for 1% -> 9% of each run, Pallas kernels for 0% -> 0%
where the time goes in v1:
time: 873 us; the launch traced here: 871 us
  other arithmetic  400 us (46%)
  waiting for transfers between devices  211 us (24%)
  local copies, waits for them, and re-layouts  96.9 us (11%)
  starting transfers between devices  68.6 us (8%)
  blocking collectives  61.7 us (7%)
  matrix products  19.2 us (2%)
  between operations  14.4 us (2%)
    scatter-add x1, other arithmetic, shards(): jnp.zeros((side * side, side), jnp.float32).at[rows_idx].add(data_rows)  195 us
    reduce_scatter x1, waiting for transfers between devices, shards(): lax.psum_scatter(volume, ('dp', 'orient'), scatter_dimension=0, tiled=True)  181 us
    scatter-add x1, other arithmetic, shards(): jnp.zeros((side * side, side), jnp.float32).at[rows_idx].add(weight_rows)  178 us
    ppermute x8, starting transfers between devices, start_notes(): clean = ppermute(clean, mesh_ax, gallery)  61.3 us
    dynamic_update_slice x8, local copies, waits for them, and re-layouts, start_notes(): lax.dynamic_update_slice_in_dim(e_next, clean, (z1 - rr) % odd * new, axi...  36.2 us
    dynamic_update_slice x7, local copies, waits for them, and re-layouts, start_notes(): lax.dynamic_update_slice_in_dim(e_next, ready, (z1 + rr) % odd * new, axi...  32.8 us
    pmax x1, blocking collectives, shards(): peak = lax.pmax(jnp.max(scores, axis=1), 'orient')  32.1 us
    psum x1, blocking collectives, shards(): total = lax.psum(jnp.sum(expo, axis=1), 'orient')  29.7 us
  transfers between devices with their start and end apart: 16, of which 8 were waited for; matrix products, arithmetic and copies ran while one was open for 9% of the time, Pallas kernels for 0%

profile of v1, /device:TPU:0, one launch (start us, length us, event | category | flops | bytes accessed | tf_op | source)
XLA Modules:
  0.0 870.9 jit_solution(8499730739675813631)
XLA Ops:
  7.7 5.1 collective-permute-start.1
  12.8 7.1 collective-permute-done
  24.4 6.9 collective-permute-done.2
  31.3 4.6 collective-permute-start.4
  35.9 6.8 collective-permute-done.4
  42.7 6.6 collective-permute-start.6
  49.3 4.7 collective-permute-done.6
  54.0 9.5 %collective-permute-start.8 = (bf16[12,16384]{1,0:T(8,128)(2,1)S(1)}, bf16[12,16384]{1,0:T(8,128)(2,1)S(1)}, u32[]{:S(2)}, u32[]{:S(2)}) collective-permute-start(bf16[12,16384]{1,0:T(8,128)(2,1)S(1)} %collective-permute-done.6), channel_id=1, source_target_pairs={{0,1},{1,2},{2,3},{3,4},{4,5},{5,6},{6,7},{7,8},{8,9},{9,10},{10,1... | collective-permute-start | bytes 1179656 | tf_op jit(solution)/shard_map/ppermute | solution.py:18
  65.4 12.3 %collective-permute-start.10 = (bf16[12,16384]{1,0:T(8,128)(2,1)S(1)}, bf16[12,16384]{1,0:T(8,128)(2,1)S(1)}, u32[]{:S(2)}, u32[]{:S(2)}) collective-permute-start(bf16[12,16384]{1,0:T(8,128)(2,1)S(1)} %collective-permute-done.8), channel_id=1, source_target_pairs={{0,1},{1,2},{2,3},{3,4},{4,5},{5,6},{6,7},{7,8},{8,9},{9,10},{10,1... | collective-permute-start | bytes 1179656 | tf_op jit(solution)/shard_map/ppermute | solution.py:18
  79.3 12.7 %collective-permute-start.12 = (bf16[12,16384]{1,0:T(8,128)(2,1)S(1)}, bf16[12,16384]{1,0:T(8,128)(2,1)}, u32[]{:S(2)}, u32[]{:S(2)}) collective-permute-start(bf16[12,16384]{1,0:T(8,128)(2,1)S(1)} %collective-permute-done.10), channel_id=1, source_target_pairs={{0,1},{1,2},{2,3},{3,4},{4,5},{5,6},{6,7},{7,8},{8,9},{9,10},{10,1... | collective-permute-start | bytes 1179656 | tf_op jit(solution)/shard_map/ppermute | solution.py:18
  93.7 12.6 %collective-permute-start.14 = (bf16[12,16384]{1,0:T(8,128)(2,1)}, bf16[12,16384]{1,0:T(8,128)(2,1)}, u32[]{:S(2)}, u32[]{:S(2)}) collective-permute-start(bf16[12,16384]{1,0:T(8,128)(2,1)} %collective-permute-done.12), channel_id=1, source_target_pairs={{0,1},{1,2},{2,3},{3,4},{4,5},{5,6},{6,7},{7,8},{8,9},{9,10},{10,1... | collective-permute-start | bytes 1179656 | tf_op jit(solution)/shard_map/ppermute | solution.py:18
  106.2 5.7 fusion.2
  115.5 4.6 dynamic_update_slice.48
  123.7 4.6 dynamic_update_slice.50
  128.3 4.6 dynamic_update_slice.51
  142.0 4.8 dynamic_update_slice.54
  146.8 4.8 dynamic_update_slice.55
  151.6 4.8 dynamic_update_slice.56
  170.0 4.8 dynamic_update_slice.60
  174.8 4.8 dynamic_update_slice.61
  179.6 4.8 dynamic_update_slice.62
  184.4 4.8 dynamic_update_slice.63
  189.2 8.2 fusion.22
  197.4 32.1 %pmax.7 = f32[192]{0:T(256)S(1)} all-reduce(f32[192]{0:T(256)S(1)} %get-tuple-element.4), channel_id=1, replica_groups=mesh['dp'=2,'orient'=16] {'orient'}, use_global_device_ids=true, to_apply=%region_2.3 | all-reduce | flops 192 | bytes 1536 | tf_op jit(solution)/shard_map/pmax | solution.py:43
  229.6 29.7 %psum.7 = f32[192]{0:T(256)S(1)} all-reduce(f32[192]{0:T(256)S(1)} %fusion.16), channel_id=1, replica_groups=mesh['dp'=2,'orient'=16] {'orient'}, use_global_device_ids=true, to_apply=%region_4.5 | all-reduce | flops 192 | bytes 1536 | tf_op jit(solution)/shard_map/psum | solution.py:45
  259.3 11.0 %fusion.17 = f32[256,16384]{1,0:T(8,128)} fusion(bf16[192,16384]{1,0:T(8,128)(2,1)} %dynamic_update_slice.63, f32[192,256]{1,0:T(8,128)S(1)} %get-tuple-element.5, f32[192]{0:T(256)S(1)} %psum.7, f32[192]{0:T(256)S(1)} %pmax.7), kind=kOutput, calls=%fused_computation.23 | convolution fusion | flops 1610760192 | bytes 23266816 | tf_op jit(solution)/shard_map/dot_general | solution.py:49
  270.4 18.0 %reshape.54 = f32[32768,128]{1,0:T(8,128)} reshape(f32[256,16384]{1,0:T(8,128)} %fusion.17) | data formatting | bytes 33554432 | tf_op jit(solution)/shard_map/reshape | solution.py:53
  288.6 8.4 bitcast_multiply_fusion
  297.0 177.9 %scatter_custom_fusion.1 = f32[16384,128]{1,0:T(8,128)} fusion(s32[32768]{0:T(1024)S(1)} %bitcast.14, f32[32768,128]{1,0:T(8,128)} %bitcast_multiply_fusion, f32[]{:T(128)} %constant.95.clone.1), kind=kCustom, calls=%fused_computation.14 | custom fusion | flops 4194304 | bytes 8389120 | tf_op jit(solution)/shard_map/scatter-add | solution.py:58
  474.9 194.9 %scatter_custom_fusion = f32[16384,128]{1,0:T(8,128)} fusion(s32[32768]{0:T(1024)S(1)} %bitcast.15, f32[32768,128]{1,0:T(8,128)} %reshape.54, f32[32768]{0:T(1024)S(1)} %bitcast.10, f32[]{:T(128)} %constant.95.clone.1), kind=kCustom, calls=%fused_computation.9 | custom fusion | flops 8388608 | bytes 25296900 | tf_op jit(solution)/shard_map/scatter-add | solution.py:54
  669.8 11.3 %pad_maximum_fusion = f32[16384,256]{1,0:T(8,128)} fusion(f32[16384,128]{1,0:T(8,128)} %scatter_custom_fusion.1, f32[16384,128]{1,0:T(8,128)} %scatter_custom_fusion), kind=kLoop, calls=%fused_computation.7 | loop fusion | flops 4194304 | bytes 33554432 | tf_op jit(solution)/shard_map/concatenate | solution.py:59
  681.1 181.1 %reduce-scatter.2.cloned.1.call-done = f32[512,256]{1,0:T(8,128)} async-done(((f32[16384,256]{1,0:T(8,128)}), f32[512,256]{1,0:T(8,128)}) %reduce-scatter.2.cloned.1.call-update) | async-done | bytes 524304 | tf_op jit(solution)/shard_map/reduce_scatter | solution.py:60
  (58 shorter events, 42.1 us)
Async XLA Ops:
  7.2 108.3 %copy-start.1 = (bf16[12,16384]{1,0:T(8,128)(2,1)S(1)}, bf16[12,16384]{1,0:T(8,128)(2,1)}, u32[]{:S(2)}) copy-start(bf16[12,16384]{1,0:T(8,128)(2,1)} %param.5) | copy-start | bytes 1179652
  7.2 855.1 %reduce-scatter.2.cloned.1.call-start = ((), (), s32[]{:S(2)}) async-start(), calls=%async_computation.1 | async-start | bytes 17301504 | tf_op jit(solution)/shard_map/reduce_scatter | solution.py:60
  7.2 12.7 %collective-permute-start = (bf16[12,16384]{1,0:T(8,128)(2,1)}, bf16[12,16384]{1,0:T(8,128)(2,1)S(1)}, u32[]{:S(2)}, u32[]{:S(2)}) collective-permute-start(bf16[12,16384]{1,0:T(8,128)(2,1)} %param.5), channel_id=1, source_target_pairs={{0,1},{1,2},{2,3},{3,4},{4,5},{5,6},{6,7},{7,8},{8,9},{9,10},{10,1... | collective-permute-start | bytes 1179656 | tf_op jit(solution)/shard_map/ppermute | solution.py:18
  7.7 14.7 %collective-permute-start.1 = (bf16[12,16384]{1,0:T(8,128)(2,1)}, bf16[12,16384]{1,0:T(8,128)(2,1)S(1)}, u32[]{:S(2)}, u32[]{:S(2)}) collective-permute-start(bf16[12,16384]{1,0:T(8,128)(2,1)} %param.5), channel_id=1, source_target_pairs={{0,15},{1,0},{2,1},{3,2},{4,3},{5,4},{6,5},{7,6},{8,7},{9,8},{10,9... | collective-permute-start | bytes 1179656 | tf_op jit(solution)/shard_map/ppermute | solution.py:21
  19.9 11.4 %collective-permute-start.2 = (bf16[12,16384]{1,0:T(8,128)(2,1)S(1)}, bf16[12,16384]{1,0:T(8,128)(2,1)S(1)}, u32[]{:S(2)}, u32[]{:S(2)}) collective-permute-start(bf16[12,16384]{1,0:T(8,128)(2,1)S(1)} %collective-permute-done), channel_id=1, source_target_pairs={{0,1},{1,2},{2,3},{3,4},{4,5},{5,6},{6,7},{7,8},{8,9},{9,10},{10,1... | collective-permute-start | bytes 1179656 | tf_op jit(solution)/shard_map/ppermute | solution.py:18
  22.4 13.5 %collective-permute-start.3 = (bf16[12,16384]{1,0:T(8,128)(2,1)S(1)}, bf16[12,16384]{1,0:T(8,128)(2,1)S(1)}, u32[]{:S(2)}, u32[]{:S(2)}) collective-permute-start(bf16[12,16384]{1,0:T(8,128)(2,1)S(1)} %collective-permute-done.1), channel_id=1, source_target_pairs={{0,15},{1,0},{2,1},{3,2},{4,3},{5,4},{6,5},{7,6},{8,7},{9,8},{10,9... | collective-permute-start | bytes 1179656 | tf_op jit(solution)/shard_map/ppermute | solution.py:21
  31.3 11.4 %collective-permute-start.4 = (bf16[12,16384]{1,0:T(8,128)(2,1)S(1)}, bf16[12,16384]{1,0:T(8,128)(2,1)S(1)}, u32[]{:S(2)}, u32[]{:S(2)}) collective-permute-start(bf16[12,16384]{1,0:T(8,128)(2,1)S(1)} %collective-permute-done.2), channel_id=1, source_target_pairs={{0,1},{1,2},{2,3},{3,4},{4,5},{5,6},{6,7},{7,8},{8,9},{9,10},{10,1... | collective-permute-start | bytes 1179656 | tf_op jit(solution)/shard_map/ppermute | solution.py:18
  35.9 13.5 %collective-permute-start.5 = (bf16[12,16384]{1,0:T(8,128)(2,1)S(1)}, bf16[12,16384]{1,0:T(8,128)(2,1)S(1)}, u32[]{:S(2)}, u32[]{:S(2)}) collective-permute-start(bf16[12,16384]{1,0:T(8,128)(2,1)S(1)} %collective-permute-done.3), channel_id=1, source_target_pairs={{0,15},{1,0},{2,1},{3,2},{4,3},{5,4},{6,5},{7,6},{8,7},{9,8},{10,9... | collective-permute-start | bytes 1179656 | tf_op jit(solution)/shard_map/ppermute | solution.py:21
  42.7 11.3 %collective-permute-start.6 = (bf16[12,16384]{1,0:T(8,128)(2,1)S(1)}, bf16[12,16384]{1,0:T(8,128)(2,1)S(1)}, u32[]{:S(2)}, u32[]{:S(2)}) collective-permute-start(bf16[12,16384]{1,0:T(8,128)(2,1)S(1)} %collective-permute-done.4), channel_id=1, source_target_pairs={{0,1},{1,2},{2,3},{3,4},{4,5},{5,6},{6,7},{7,8},{8,9},{9,10},{10,1... | collective-permute-start | bytes 1179656 | tf_op jit(solution)/shard_map/ppermute | solution.py:18
  49.3 4.7 copy-start.2
  49.3 14.2 %collective-permute-start.7 = (bf16[12,16384]{1,0:T(8,128)(2,1)S(1)}, bf16[12,16384]{1,0:T(8,128)(2,1)S(1)}, u32[]{:S(2)}, u32[]{:S(2)}) collective-permute-start(bf16[12,16384]{1,0:T(8,128)(2,1)S(1)} %collective-permute-done.5), channel_id=1, source_target_pairs={{0,15},{1,0},{2,1},{3,2},{4,3},{5,4},{6,5},{7,6},{8,7},{9,8},{10,9... | collective-permute-start | bytes 1179656 | tf_op jit(solution)/shard_map/ppermute | solution.py:21
  54.0 9.5 %copy-start.3 = (bf16[12,16384]{1,0:T(8,128)(2,1)}, bf16[12,16384]{1,0:T(8,128)(2,1)S(1)}, u32[]{:S(2)}) copy-start(bf16[12,16384]{1,0:T(8,128)(2,1)S(1)} %collective-permute-done.6) | copy-start | bytes 1179652
  54.0 11.4 %collective-permute-start.8 = (bf16[12,16384]{1,0:T(8,128)(2,1)S(1)}, bf16[12,16384]{1,0:T(8,128)(2,1)S(1)}, u32[]{:S(2)}, u32[]{:S(2)}) collective-permute-start(bf16[12,16384]{1,0:T(8,128)(2,1)S(1)} %collective-permute-done.6), channel_id=1, source_target_pairs={{0,1},{1,2},{2,3},{3,4},{4,5},{5,6},{6,7},{7,8},{8,9},{9,10},{10,1... | collective-permute-start | bytes 1179656 | tf_op jit(solution)/shard_map/ppermute | solution.py:18
  63.6 1.9 copy-start.4
  63.6 14.2 %collective-permute-start.9 = (bf16[12,16384]{1,0:T(8,128)(2,1)S(1)}, bf16[12,16384]{1,0:T(8,128)(2,1)S(1)}, u32[]{:S(2)}, u32[]{:S(2)}) collective-permute-start(bf16[12,16384]{1,0:T(8,128)(2,1)S(1)} %collective-permute-done.7), channel_id=1, source_target_pairs={{0,15},{1,0},{2,1},{3,2},{4,3},{5,4},{6,5},{7,6},{8,7},{9,8},{10,9... | collective-permute-start | bytes 1179656 | tf_op jit(solution)/shard_map/ppermute | solution.py:21
  65.4 12.4 %copy-start.5 = (bf16[12,16384]{1,0:T(8,128)(2,1)}, bf16[12,16384]{1,0:T(8,128)(2,1)S(1)}, u32[]{:S(2)}) copy-start(bf16[12,16384]{1,0:T(8,128)(2,1)S(1)} %collective-permute-done.8) | copy-start | bytes 1179652
  65.4 13.9 %collective-permute-start.10 = (bf16[12,16384]{1,0:T(8,128)(2,1)S(1)}, bf16[12,16384]{1,0:T(8,128)(2,1)S(1)}, u32[]{:S(2)}, u32[]{:S(2)}) collective-permute-start(bf16[12,16384]{1,0:T(8,128)(2,1)S(1)} %collective-permute-done.8), channel_id=1, source_target_pairs={{0,1},{1,2},{2,3},{3,4},{4,5},{5,6},{6,7},{7,8},{8,9},{9,10},{10,1... | collective-permute-start | bytes 1179656 | tf_op jit(solution)/shard_map/ppermute | solution.py:18
  77.8 1.5 copy-start.7
  77.8 15.3 %collective-permute-start.11 = (bf16[12,16384]{1,0:T(8,128)(2,1)S(1)}, bf16[12,16384]{1,0:T(8,128)(2,1)}, u32[]{:S(2)}, u32[]{:S(2)}) collective-permute-start(bf16[12,16384]{1,0:T(8,128)(2,1)S(1)} %collective-permute-done.9), channel_id=1, source_target_pairs={{0,15},{1,0},{2,1},{3,2},{4,3},{5,4},{6,5},{7,6},{8,7},{9,8},{10,9... | collective-permute-start | bytes 1179656 | tf_op jit(solution)/shard_map/ppermute | solution.py:21
  79.3 13.7 %copy-start.9 = (bf16[12,16384]{1,0:T(8,128)(2,1)}, bf16[12,16384]{1,0:T(8,128)(2,1)S(1)}, u32[]{:S(2)}) copy-start(bf16[12,16384]{1,0:T(8,128)(2,1)S(1)} %collective-permute-done.10) | copy-start | bytes 1179652
  79.3 14.4 %collective-permute-start.12 = (bf16[12,16384]{1,0:T(8,128)(2,1)S(1)}, bf16[12,16384]{1,0:T(8,128)(2,1)}, u32[]{:S(2)}, u32[]{:S(2)}) collective-permute-start(bf16[12,16384]{1,0:T(8,128)(2,1)S(1)} %collective-permute-done.10), channel_id=1, source_target_pairs={{0,1},{1,2},{2,3},{3,4},{4,5},{5,6},{6,7},{7,8},{8,9},{9,10},{10,1... | collective-permute-start | bytes 1179656 | tf_op jit(solution)/shard_map/ppermute | solution.py:18
  93.1 86.5 %collective-permute-start.13 = (bf16[12,16384]{1,0:T(8,128)(2,1)}, bf16[12,16384]{1,0:T(8,128)(2,1)}, u32[]{:S(2)}, u32[]{:S(2)}) collective-permute-start(bf16[12,16384]{1,0:T(8,128)(2,1)} %collective-permute-done.11), channel_id=1, source_target_pairs={{0,15},{1,0},{2,1},{3,2},{4,3},{5,4},{6,5},{7,6},{8,7},{9,8},{10,9... | collective-permute-start | bytes 1179656 | tf_op jit(solution)/shard_map/ppermute | solution.py:21
  93.7 90.7 %collective-permute-start.14 = (bf16[12,16384]{1,0:T(8,128)(2,1)}, bf16[12,16384]{1,0:T(8,128)(2,1)}, u32[]{:S(2)}, u32[]{:S(2)}) collective-permute-start(bf16[12,16384]{1,0:T(8,128)(2,1)} %collective-permute-done.12), channel_id=1, source_target_pairs={{0,1},{1,2},{2,3},{3,4},{4,5},{5,6},{6,7},{7,8},{8,9},{9,10},{10,1... | collective-permute-start | bytes 1179656 | tf_op jit(solution)/shard_map/ppermute | solution.py:18
  115.5 73.7 %copy-start.11 = (f32[128,128]{1,0:T(8,128)S(1)}, f32[128,128]{1,0:T(8,128)}, u32[]{:S(2)}) copy-start(f32[128,128]{1,0:T(8,128)} %param.9) | copy-start | bytes 196612
  120.1 36.3 %copy-start.6 = (bf16[12,16384]{1,0:T(8,128)(2,1)S(1)}, bf16[12,16384]{1,0:T(8,128)(2,1)}, u32[]{:S(2)}) copy-start(bf16[12,16384]{1,0:T(8,128)(2,1)} %copy-done.5) | copy-start | bytes 1179652
  123.7 37.2 %copy-start.8 = (bf16[12,16384]{1,0:T(8,128)(2,1)S(1)}, bf16[12,16384]{1,0:T(8,128)(2,1)}, u32[]{:S(2)}) copy-start(bf16[12,16384]{1,0:T(8,128)(2,1)} %copy-done.7) | copy-start | bytes 1179652
  128.3 37.1 %copy-start.10 = (bf16[12,16384]{1,0:T(8,128)(2,1)S(1)}, bf16[12,16384]{1,0:T(8,128)(2,1)}, u32[]{:S(2)}) copy-start(bf16[12,16384]{1,0:T(8,128)(2,1)} %copy-done.9) | copy-start | bytes 1179652
  270.4 18.0 %copy-start = (f32[256,128]{1,0:T(8,128)S(1)}, f32[256,128]{1,0:T(8,128)}, u32[]{:S(2)}) copy-start(f32[256,128]{1,0:T(8,128)} %param.8) | copy-start | bytes 393220
Sparse Core Ops, SparseCore 0:
  681.2 180.9 reduce-scatter.1
